TPU v7x, 32 devices: a whole 2x2x4 slice. The times are simulated.
32 devices in a mesh: dom: 16 (over z, y, x), orb: 2 (over core).
Axes of the slice: x: 2, y: 2, z: 4, core: 2. Of those that a mesh axis runs over, the one named last changes fastest.
Arguments:
- block: float32 [256, 10816], P('orb', 'dom')
- conn: int32 [125, 144], P(None, 'dom'), may hold values from 0 to 844, as said below
- bottom: int32 [2704], P('dom'), may hold values from 0 to 675, as said below
- cell_scale: float32 [144], P('dom'), may hold values from 0.5 to 2
- potential: float32 [216, 144], P(None, 'dom'), may hold values from 0.1 to 1
- mass: float32 [10816], P('dom'), may hold values from 0.5 to 2
- stiffness: float32 [125, 125], replicated, as said below
- interp: float32 [216, 125], replicated, may hold values from -0.5 to 0.5
- occupancy: float32 [256], P('orb'), may hold values from 0.2 to 2
- spectrum: float32 [2], replicated, as said below
Outputs:
- density: float32 [216, 144], P(None, 'dom')
Inputs may be any that keep to these rules, and one draw needn't show every extreme that they name: `conn`: for the cells of domain d an entry below 676 is one of d's own local node numbers and 676 + f names entry f of the next domain's list in bottom; every own node is named by some cell of its domain, and the cells form a conforming mesh. `bottom`: each domain's 169 entries are distinct local numbers of its own nodes. `stiffness`: symmetric and positive definite. spectrum[0] < spectrum[1].
All inputs are finite; a program needn't handle non-finite values.
Results may differ from a plain program's by a relative error of at most 0.0001.
Values sent between devices are 32-bit elements; how exact they have to be, the bound alone decides.
A program may use at most 64 MiB of HBM per device.

v0:
```python
import functools

import jax
import jax.numpy as jnp
from jax import lax
from jax.experimental import pallas as pl
from jax.experimental.pallas import tpu as pltpu
from jax.sharding import PartitionSpec as P

DEG = 3
LANE = 128
PAD = 256
HI = lax.Precision.HIGHEST
MESH = pl.DeviceIdType.MESH
F32 = jnp.float32
BF16 = jnp.bfloat16
NN = (((1,), (0,)), ((), ()))
NT = (((1,), (1,)), ((), ()))
TN = (((0,), (0,)), ((), ()))
VLIMIT = 48 * 1024 * 1024


def up(value, unit):
    return -(-value // unit) * unit


def full_dot(left, right, dims=NN):
    return lax.dot_general(left, right, dims, precision=HI, preferred_element_type=F32)


def split2(value):
    high = value.astype(BF16)
    return high, (value - high.astype(F32)).astype(BF16)


def part_dot(left, right, dims=NN):
    return lax.dot_general(left, right, dims, preferred_element_type=F32)


def dot3(left, right, dims=NN):
    high, low = left
    main, rest = right
    return (part_dot(low, main, dims) + part_dot(high, rest, dims)) + part_dot(high, main, dims)


def pick_dot(parts, onehot, dims=NN):
    high, low = parts
    return part_dot(low, onehot, dims) + part_dot(high, onehot, dims)


def assemble_kernel(
    conn_ref, scale_ref, pot_ref, stiff_ref, interp_ref, ah_ref, al_ref, gt_ref, w_ref, k_ref, b_ref
):
    ext = ah_ref.shape[0]
    cells = conn_ref.shape[0]
    npc = stiff_ref.shape[0]
    k_ref[...] = jnp.zeros_like(k_ref)
    k_ref[:npc, :npc] = stiff_ref[...]
    b_ref[...] = jnp.zeros_like(b_ref)
    b_ref[:, :npc] = interp_ref[...]
    interp = b_ref[...]
    parts = split2(interp)
    rows = lax.broadcasted_iota(jnp.int32, (ext, LANE), 0)
    for cell in range(cells):
        cols = slice(cell * LANE, (cell + 1) * LANE)
        hot = (rows == conn_ref[cell : cell + 1, :]).astype(F32).astype(BF16)
        gt_ref[:, cols] = hot
        local = dot3(parts, split2(interp * pot_ref[:, cell : cell + 1]), TN)
        local = local + k_ref[...] * scale_ref[0:1, cell : cell + 1]
        both = part_dot(hot, jnp.concatenate(split2(local), axis=1)).astype(BF16)
        w_ref[0, :, cols] = both[:, :LANE]
        w_ref[1, :, cols] = both[:, LANE:]
    for first in range(0, ext, PAD):
        for second in range(first, ext, PAD):
            here, there = slice(first, first + PAD), slice(second, second + PAD)
            hot = gt_ref[there, :]
            block = part_dot(w_ref[1, here, :], hot, NT) + part_dot(w_ref[0, here, :], hot, NT)
            ah_ref[here, there], al_ref[here, there] = split2(block)
            if second > first:
                ah_ref[there, here], al_ref[there, here] = split2(block.T)


def filter_kernel(
    ndom,
    fits,
    node_dev,
    spec_ref,
    v_ref,
    ah_ref,
    al_ref,
    bottom_ref,
    mass_ref,
    occ_ref,
    vall_out,
    gram_out,
    occ_out,
    cur,
    prev,
    vb,
    rb,
    gslot,
    rslot,
    kp,
    edge_block,
    mass_row,
    bottom_row,
    vall,
    occs,
    gp,
    rs,
    gall,
    fsend,
    frecv,
    rsend,
    rrecv,
    ksem,
    psend,
    precv,
    ssend,
    srecv,
    gsend,
    grecv,
):
    d = lax.axis_index("dom")
    o = lax.axis_index("orb")
    other = 1 - o
    own = v_ref.shape[0]
    nodes = cur.shape[1]
    has_prev = d > 0
    has_next = d < ndom - 1
    before = lax.rem(d + ndom - 1, ndom)
    after = lax.rem(d + 1, ndom)

    gslot[...] = jnp.zeros_like(gslot)
    rslot[...] = jnp.zeros_like(rslot)
    kp[...] = jnp.zeros_like(kp)
    edge_block[...] = ah_ref[nodes:, nodes:].astype(F32) + al_ref[nodes:, nodes:].astype(F32)

    barrier = pltpu.get_barrier_semaphore()
    pl.semaphore_signal(
        barrier, inc=1, device_id={"dom": d, "orb": other}, device_id_type=MESH
    )
    if fits:

        def greet(k, carry):
            pl.semaphore_signal(
                barrier,
                inc=1,
                device_id={"dom": lax.rem(d + k, ndom), "orb": o},
                device_id_type=MESH,
            )
            return carry

        lax.fori_loop(1, ndom, greet, 0)
        pl.semaphore_wait(barrier, ndom)
    else:
        for ok, peer in ((has_prev, before), (has_next, after)):

            @pl.when(ok)
            def _():
                pl.semaphore_signal(
                    barrier, inc=1, device_id={"dom": peer, "orb": o}, device_id_type=MESH
                )
                pl.semaphore_wait(barrier, 1)

        pl.semaphore_wait(barrier, 1)

    def remote(src, dst, send, recv, dom, orb):
        return pltpu.make_async_remote_copy(
            src_ref=src,
            dst_ref=dst,
            send_sem=send,
            recv_sem=recv,
            device_id={"dom": dom, "orb": orb},
            device_id_type=MESH,
        )

    def face(step):
        return remote(
            vb.at[step], gslot.at[step], fsend.at[step], frecv.at[step], before, o
        )

    def rim(step):
        return remote(rb.at[step], rslot.at[step], rsend.at[step], rrecv.at[step], after, o)

    corner = remote(
        edge_block, kp, ksem.at[0], ksem.at[1], after, o
    )

    @pl.when(has_next)
    def _():
        corner.start()

    occs[o] = jnp.broadcast_to(occ_ref[...], occs.shape[1:])
    occ_copy = remote(occs.at[o], occs.at[o], psend.at[0], precv.at[0], d, other)
    occ_copy.start()

    halfwidth = (spec_ref[1] - spec_ref[0]) / 2.0
    centre = (spec_ref[1] + spec_ref[0]) / 2.0
    cur[...] = jnp.zeros_like(cur)
    cur[:, :node_dev] = v_ref[...]
    mass_row[...] = jnp.ones_like(mass_row)
    mass_row[:, :node_dev] = mass_ref[...]
    bottom_row[...] = jnp.full_like(bottom_row, -1)
    bottom_row[:, : bottom_ref.shape[1]] = bottom_ref[...]
    mass = mass_row[...]
    over_mass = 1.0 / (mass * halfwidth)
    shift = centre / halfwidth
    hot = (
        lax.broadcasted_iota(jnp.int32, (nodes, PAD), 0) == bottom_row[...]
    ).astype(F32).astype(BF16)

    for step in range(DEG):
        value = cur[...]
        parts = split2(value)
        edge = pick_dot(parts, hot)
        vb[step] = edge

        @pl.when(has_prev)
        def _():
            face(step).start()

        rb[step] = dot3(parts, (ah_ref[:nodes, nodes:], al_ref[:nodes, nodes:]))

        @pl.when(has_next)
        def _():
            rim(step).start()

        total = dot3(parts, (ah_ref[:nodes, :nodes], al_ref[:nodes, :nodes]))
        if step == 0:

            @pl.when(has_prev)
            def _():
                corner.wait_recv()

        extra = dot3(split2(edge), split2(kp[...]))

        @pl.when(has_next)
        def _():
            face(step).wait_recv()

        @pl.when(has_prev)
        def _():
            rim(step).wait_recv()

        total = total + dot3(
            split2(gslot[step]), (ah_ref[nodes:, :nodes], al_ref[nodes:, :nodes])
        )
        total = total + pick_dot(split2(extra + rslot[step]), hot, NT)
        applied = total * over_mass - shift * value
        if step > 0:
            applied = 2.0 * applied - prev[...]
        prev[...] = value
        cur[...] = applied

    value = cur[...]
    vall[o, :, :nodes] = value
    half = remote(
        vall.at[o, :, pl.ds(0, nodes)],
        vall.at[o, :, pl.ds(0, nodes)],
        psend.at[1],
        precv.at[1],
        d,
        other,
    )
    half.start()
    vb[DEG] = pick_dot(split2(value), hot)

    @pl.when(has_prev)
    def _():
        face(DEG).start()

    weighted = value * mass
    gp[o] = full_dot(weighted, value, NT)
    half.wait_recv()
    gp[other] = full_dot(weighted, vall[other, :, :nodes], NT)

    @pl.when(has_next)
    def _():
        face(DEG).wait_recv()

    vall[o, :, nodes:] = gslot[DEG]
    ghost = remote(
        vall.at[o, :, pl.ds(nodes, PAD)],
        vall.at[o, :, pl.ds(nodes, PAD)],
        psend.at[2],
        precv.at[2],
        d,
        other,
    )
    ghost.start()

    if fits:
        share = own // ndom

        def scatter(k):
            peer = lax.rem(d + k, ndom)
            return remote(
                gp.at[:, pl.ds(pl.multiple_of(peer * share, 8), share), :],
                rs.at[k],
                ssend.at[k],
                srecv.at[k],
                peer,
                o,
            )

        mine = pl.ds(pl.multiple_of(d * share, 8), share)

        def gather(k):
            return remote(
                gall.at[o, :, mine, :],
                gall.at[o, :, mine, :],
                gsend.at[k],
                grecv.at[k],
                lax.rem(d + k, ndom),
                o,
            )

        def arrive(k):
            came = lax.rem(d + ndom - k, ndom)
            spot = pl.ds(pl.multiple_of(came * share, 8), share)
            return remote(
                gall.at[o, :, spot, :],
                gall.at[o, :, spot, :],
                gsend.at[k],
                grecv.at[k],
                came,
                o,
            )

        def run(action):
            lax.fori_loop(1, ndom, lambda k, carry: (action(k), carry)[1], 0)

        run(lambda k: scatter(k).start())
        run(lambda k: scatter(k).wait_recv())
        rs[0] = gp[:, mine, :]
        total = rs[0]
        for k in range(1, ndom):
            total = total + rs[k]
        gall[o, :, mine, :] = total / (ndom * node_dev)
        run(lambda k: gather(k).start())
        run(lambda k: arrive(k).wait_recv())
        swap = remote(gall.at[o], gall.at[o], psend.at[3], precv.at[3], d, other)
        swap.start()
        swap.wait_recv()
        for row in range(2):
            for col in range(2):
                gram_out[row * own : (row + 1) * own, col * own : (col + 1) * own] = gall[
                    row, col
                ]
        run(lambda k: scatter(k).wait_send())
        run(lambda k: gather(k).wait_send())
        swap.wait_send()
    else:
        whole = [vall[0, :, :nodes], vall[1, :, :nodes]]
        for row in range(2):
            for col in range(2):
                gram_out[row * own : (row + 1) * own, col * own : (col + 1) * own] = full_dot(
                    whole[row] * mass, whole[col], NT
                )

    ghost.wait_recv()
    occ_copy.wait_recv()
    vall_out[...] = vall[...]
    occ_out[...] = occs[...]
    occ_copy.wait_send()
    half.wait_send()
    ghost.wait_send()
    for step in range(DEG + 1):

        @pl.when(has_prev)
        def _():
            face(step).wait_send()

    for step in range(DEG):

        @pl.when(has_next)
        def _():
            rim(step).wait_send()

    @pl.when(has_next)
    def _():
        corner.wait_send()


def small_inverse(tile, side, size, filler):
    lanes = lax.broadcasted_iota(jnp.int32, tile.shape, 1)
    rows = lax.broadcasted_iota(jnp.int32, tile.shape, 0)
    keep = (lanes >= side * size) & (lanes < (side + 1) * size)
    unit = (lanes - (1 - side) * size == rows).astype(F32)
    work = jnp.where(keep, tile, unit)
    groups = size // 8
    pieces = [work[8 * g : 8 * g + 8] for g in range(groups)]
    below = lax.broadcasted_iota(jnp.int32, (8, LANE), 0)
    panel = 4
    full = (8, LANE)
    for start in range(0, size, panel):
        top, row = divmod(start, 8)
        lane = side * size + start
        head = [pieces[top][row + a : row + a + 1, :] for a in range(panel)]
        line = [jnp.broadcast_to(value, full) for value in head]
        pivot = [
            [
                jnp.broadcast_to(head[a][:, lane + b : lane + b + 1], full) if b >= a else None
                for b in range(panel)
            ]
            for a in range(panel)
        ]
        column = [
            [
                jnp.broadcast_to(pieces[g][:, lane + b : lane + b + 1], full)
                for b in range(panel)
            ]
            for g in range(top, groups)
        ]
        for a in range(panel):
            over = 1.0 / pivot[a][a]
            for g in range(top, groups):
                if g == top and row + a == 7:
                    continue
                terms = column[g - top]
                factor = terms[a] * over
                if g == top:
                    factor = jnp.where(below > row + a, factor, 0.0)
                pieces[g] = pieces[g] - factor * line[a]
                for b in range(a + 1, panel):
                    terms[b] = terms[b] - factor * pivot[a][b]
            for b in range(a + 1, panel):
                factor = pivot[a][b] * over
                line[b] = line[b] - factor * line[a]
                for c in range(b, panel):
                    pivot[b][c] = pivot[b][c] - factor * pivot[a][c]
        if start // panel % 3 == 1:
            next(filler, None)
    work = jnp.concatenate(pieces, axis=0)
    diag = jnp.sum(jnp.where(lanes - side * size == rows, work, 0.0), axis=1, keepdims=True)
    work = work * (1.0 / jnp.sqrt(diag))
    return work[:, (1 - side) * size : (2 - side) * size]


def density_kernel(
    gram_ref, vall_ref, gt_ref, interp_ref, occ_ref, out_ref, w_ref, x_ref, v_ref, q_ref, b_ref
):
    orbs = gram_ref.shape[0]
    own = vall_ref.shape[1]
    cells = out_ref.shape[0]
    gauss, npc = interp_ref.shape
    size = 64
    w_ref[:, :orbs] = gram_ref[...]
    shape = (orbs, orbs)
    eye = lax.broadcasted_iota(jnp.int32, shape, 0) == lax.broadcasted_iota(jnp.int32, shape, 1)
    w_ref[:, orbs:] = eye.astype(F32)
    b_ref[...] = jnp.zeros_like(b_ref)
    b_ref[:, :npc] = interp_ref[...]
    basis = split2(b_ref[...])
    for half in range(2):
        part = slice(half * own, (half + 1) * own)
        v_ref[0, part, :], v_ref[1, part, :] = split2(vall_ref[half])

    def quadrature():
        for cell in range(cells):
            local = pick_dot(
                (v_ref[0], v_ref[1]), gt_ref[:, cell * LANE : (cell + 1) * LANE]
            )
            yield
            q_ref[0, cell], q_ref[1, cell] = split2(dot3(split2(local), basis, NT))
            yield

    filler = quadrature()
    for first in range(0, orbs, size):
        last = first + size
        base = first // LANE * LANE
        tile = w_ref[first:last, base : base + LANE]
        lower = small_inverse(tile, (first - base) // size, size, filler)
        step = full_dot(lower, w_ref[first:last, :])
        x_ref[first:last, :] = step[:, orbs:]
        if last < orbs:
            w_ref[last:, :] = w_ref[last:, :] - full_dot(step[:, last:orbs], step, TN)
    for _ in filler:
        pass
    inverse = split2(x_ref[...])
    occ = jnp.concatenate([occ_ref[0, 0:1, :own], occ_ref[1, 0:1, :own]], axis=1)
    weight = jnp.sum(jnp.where(eye, occ, 0.0), axis=1, keepdims=True) / orbs
    for cell in range(cells):
        ortho = dot3(inverse, (q_ref[0, cell], q_ref[1, cell]))
        out_ref[cell : cell + 1, :] = jnp.sum(weight * (ortho * ortho), axis=0, keepdims=True)


def per_device(
    ndom, block, conn, bottom, cell_scale, potential, mass, stiffness, interp, occupancy, spectrum
):
    own, node_dev = block.shape
    npc, cells = conn.shape
    gauss = interp.shape[0]
    nodes = up(node_dev, PAD)
    ext = nodes + PAD
    orbs = 2 * own
    fits = own % (8 * ndom) == 0
    moved = jnp.where(conn >= node_dev, conn + (nodes - node_dev), conn)
    moved = jnp.pad(moved, ((0, LANE - npc), (0, 0)), constant_values=-1).T
    vm = pl.BlockSpec(memory_space=pltpu.VMEM)
    sm = pl.BlockSpec(memory_space=pltpu.SMEM)
    local_params = pltpu.CompilerParams(vmem_limit_bytes=VLIMIT)
    high, low, onehot = pl.pallas_call(
        assemble_kernel,
        name="assemble",
        out_shape=(
            jax.ShapeDtypeStruct((ext, ext), BF16),
            jax.ShapeDtypeStruct((ext, ext), BF16),
            jax.ShapeDtypeStruct((ext, cells * LANE), BF16),
        ),
        in_specs=[vm] * 5,
        out_specs=(vm, vm, vm),
        scratch_shapes=[
            pltpu.VMEM((2, ext, cells * LANE), BF16),
            pltpu.VMEM((LANE, LANE), F32),
            pltpu.VMEM((gauss, LANE), F32),
        ],
        compiler_params=local_params,
    )(moved, cell_scale[None, :], potential, stiffness, interp)

    dma = pltpu.SemaphoreType.DMA
    peers = ndom if fits else 1
    share = own // ndom if fits else 8
    vall, gram, occ = pl.pallas_call(
        functools.partial(filter_kernel, ndom, fits, node_dev),
        name="filter",
        out_shape=(
            jax.ShapeDtypeStruct((2, own, ext), F32),
            jax.ShapeDtypeStruct((orbs, orbs), F32),
            jax.ShapeDtypeStruct((2, 8, own), F32),
        ),
        in_specs=[sm] + [vm] * 6,
        out_specs=(vm, vm, vm),
        scratch_shapes=[
            pltpu.VMEM((own, nodes), F32),
            pltpu.VMEM((own, nodes), F32),
            pltpu.VMEM((DEG + 1, own, PAD), F32),
            pltpu.VMEM((DEG, own, PAD), F32),
            pltpu.VMEM((DEG + 1, own, PAD), F32),
            pltpu.VMEM((DEG, own, PAD), F32),
            pltpu.VMEM((PAD, PAD), F32),
            pltpu.VMEM((PAD, PAD), F32),
            pltpu.VMEM((1, nodes), F32),
            pltpu.VMEM((1, PAD), jnp.int32),
            pltpu.VMEM((2, own, ext), F32),
            pltpu.VMEM((2, 8, own), F32),
            pltpu.VMEM((2, own, own), F32),
            pltpu.VMEM((peers, 2, share, own), F32),
            pltpu.VMEM((2, 2, own, own), F32),
            dma((DEG + 1,)),
            dma((DEG + 1,)),
            dma((DEG,)),
            dma((DEG,)),
            dma((2,)),
            dma((4,)),
            dma((4,)),
            dma((peers,)),
            dma((peers,)),
            dma((peers,)),
            dma((peers,)),
        ],
        compiler_params=pltpu.CompilerParams(
            collective_id=0, has_side_effects=True, vmem_limit_bytes=VLIMIT
        ),
    )(spectrum, block, high, low, bottom[None, :], mass[None, :], occupancy[None, :])
    if not fits:
        gram = lax.psum(gram, "dom") / (ndom * node_dev)

    density = pl.pallas_call(
        density_kernel,
        name="density",
        out_shape=jax.ShapeDtypeStruct((cells, gauss), F32),
        in_specs=[vm] * 5,
        out_specs=vm,
        scratch_shapes=[
            pltpu.VMEM((orbs, 2 * orbs), F32),
            pltpu.VMEM((orbs, orbs), F32),
            pltpu.VMEM((2, orbs, ext), BF16),
            pltpu.VMEM((2, cells, orbs, gauss), BF16),
            pltpu.VMEM((gauss, LANE), F32),
        ],
        compiler_params=local_params,
    )(gram, vall, onehot, interp, occ)
    return density.T


def solution(mesh):
    in_specs = (
        P("orb", "dom"),
        P(None, "dom"),
        P("dom"),
        P("dom"),
        P(None, "dom"),
        P("dom"),
        P(),
        P(),
        P("orb"),
        P(),
    )
    out_specs = P(None, "dom")
    return jax.shard_map(
        functools.partial(per_device, mesh.shape["dom"]),
        mesh=mesh,
        in_specs=in_specs,
        out_specs=out_specs,
        check_vma=False,
    )
```

profile of v0, /device:TPU:1, one launch (start us, length us, event | category | flops | bytes accessed | tf_op | source)
XLA Modules:
  0.0 86.7 jit_solution(11505365382644673183)
XLA Ops:
  0.0 0.7 broadcast_in_dim.14.mass_ref
  0.7 0.7 compare_select_fusion
  1.4 0.8 copy.11.pot_ref
  2.2 1.1 %copy.12.v_ref = f32[128,676]{1,0:T(8,128)S(1)} copy(f32[128,676]{0,1:T(8,128)} %param.10) | data formatting | bytes 692224 | tf_op args[0]
  3.4 0.0 copy-start.1
  3.4 0.9 %copy-done.1 = f32[216,125]{1,0:T(8,128)S(1)} copy-done((f32[216,125]{1,0:T(8,128)S(1)}, f32[216,125]{1,0:T(8,128)}, u32[]{:S(2)}) %copy-start.1) | copy-done | bytes 108024
  4.3 0.0 copy-start.2
  4.3 0.8 copy-done.2
  5.1 0.0 copy-start.4
  5.1 0.7 copy-done.4
  5.8 6.2 %assemble.1 = (bf16[1024,1024]{1,0:T(8,128)(2,1)S(1)}, bf16[1024,1024]{1,0:T(8,128)(2,1)S(1)}, bf16[1024,1152]{1,0:T(8,128)(2,1)}) custom-call(s32[9,128]{1,0:T(8,128)S(1)} %pad_bitcast_fusion.conn_ref, f32[1,9]{1,0:T(1,128)S(1)} %bitcast.7, f32[216,9]{1,0:T(8,128)S(1)} %copy.11.pot_ref, f32[125,125]{1,0:T(8,128)S(1)} %copy-done.2, f32[216,125]{1,0:T(8,128)S(1)} %copy-done.1), custom_call_target="tpu_custom_call" | custom-call | tf_op jit(solution)/shard_map/assemble/pallas_call | solution.py:504
  12.0 0.0 copy-start.3
  12.0 0.7 copy-done.3
  12.7 0.0 copy-start.5
  12.7 0.7 copy-done.5
  13.3 0.0 copy-start.6
  13.3 0.7 copy-done.6
  14.0 0.0 copy-start
  14.0 57.4 %filter.1 = (f32[2,128,1024]{2,1,0:T(8,128)S(1)}, f32[256,256]{1,0:T(8,128)S(1)}, f32[2,8,128]{2,1,0:T(8,128)S(1)}) custom-call(f32[2]{0:T(128)S(1)} %copy-done.5, f32[128,676]{1,0:T(8,128)S(1)} %copy.12.v_ref, bf16[1024,1024]{1,0:T(8,128)(2,1)S(1)} %get-tuple-element.11.ah_ref, bf16[1024,1024]{1,0:T(8,128)(2,1)S(1)} %get-tuple-element.12.al_ref, ...), custom_call_target="tpu_custom_call" | custom-call | tf_op jit(solution)/shard_map/filter/pallas_call | solution.py:525
  71.4 0.0 copy-done
  71.4 15.3 %density.1 = f32[9,216]{1,0:T(8,128)} custom-call(f32[256,256]{1,0:T(8,128)S(1)} %get-tuple-element.13.gram_ref, f32[2,128,1024]{2,1,0:T(8,128)S(1)} %get-tuple-element.14.vall_ref, bf16[1024,1152]{1,0:T(8,128)(2,1)S(1)} %copy-done, f32[216,125]{1,0:T(8,128)S(1)} %copy-done.1, f32[2,8,128]{2,1,0:T(8,128)S(1)} %get-tuple-element.16.occ_ref), custom_call_target="tpu_custom_call" | custom-call | tf_op jit(solution)/shard_map/density/pallas_call | solution.py:570
  (1 shorter events, 0.0 us)
Async XLA Ops:
  3.4 0.9 %copy-start.1 = (f32[216,125]{1,0:T(8,128)S(1)}, f32[216,125]{1,0:T(8,128)}, u32[]{:S(2)}) copy-start(f32[216,125]{1,0:T(8,128)} %interp_ref.3) | copy-start | bytes 324004
  4.3 0.8 copy-start.2
  5.1 0.7 copy-start.4
  12.0 0.7 copy-start.3
  12.7 0.7 copy-start.5
  13.3 0.7 copy-start.6
  14.0 57.4 %copy-start = (bf16[1024,1152]{1,0:T(8,128)(2,1)S(1)}, bf16[1024,1152]{1,0:T(8,128)(2,1)}, u32[]{:S(2)}) copy-start(bf16[1024,1152]{1,0:T(8,128)(2,1)} %get-tuple-element.15.gt_ref) | copy-start | bytes 7077892
where the time goes:
time: 87 us; the launch traced here: 86.7 us
  Pallas kernels  78.9 us (91%)
  local copies, waits for them, and re-layouts  7.03 us (8%)
    pallas_call x1, Pallas kernels, per_device(): pl.pallas_call(functools.partial(filter_kernel, ndom, fits, node_dev), na...  57.4 us
    pallas_call x1, Pallas kernels, per_device(): pl.pallas_call(density_kernel, name='density', out_shape=jax.ShapeDtypeSt...  15.3 us
    unnamed x16, local copies, waits for them, and re-layouts  6.34 us
    pallas_call x1, Pallas kernels, per_device(): pl.pallas_call(assemble_kernel, name='assemble', out_shape=(jax.ShapeDtyp...  6.23 us

commit v1 on v0

v1 whole, which is shorter than its diff:
```python
import functools

import jax
import jax.numpy as jnp
from jax import lax
from jax.experimental import pallas as pl
from jax.experimental.pallas import tpu as pltpu
from jax.sharding import PartitionSpec as P

DEG = 3
LANE = 128
PAD = 256
HI = lax.Precision.HIGHEST
MESH = pl.DeviceIdType.MESH
F32 = jnp.float32
BF16 = jnp.bfloat16
NN = (((1,), (0,)), ((), ()))
NT = (((1,), (1,)), ((), ()))
TN = (((0,), (0,)), ((), ()))
TT = (((0,), (1,)), ((), ()))
VLIMIT = 48 * 1024 * 1024


def up(value, unit):
    return -(-value // unit) * unit


def full_dot(left, right, dims=NN):
    return lax.dot_general(left, right, dims, precision=HI, preferred_element_type=F32)


def split2(value):
    high = value.astype(BF16)
    return high, (value - high.astype(F32)).astype(BF16)


def part_dot(left, right, dims=NN):
    return lax.dot_general(left, right, dims, preferred_element_type=F32)


def dot3(left, right, dims=NN):
    high, low = left
    main, rest = right
    return (part_dot(low, main, dims) + part_dot(high, rest, dims)) + part_dot(high, main, dims)


def pick_dot(parts, onehot, dims=NN):
    high, low = parts
    return part_dot(low, onehot, dims) + part_dot(high, onehot, dims)


def assemble(
    conn_ref, scale_ref, pot_ref, stiff_ref, interp_ref, ah_ref, al_ref, corner_ref, gt_ref, w_ref, k_ref, b_ref
):
    ext = ah_ref.shape[0]
    cells = conn_ref.shape[0]
    npc = stiff_ref.shape[0]
    k_ref[...] = jnp.zeros_like(k_ref)
    k_ref[:npc, :npc] = stiff_ref[...]
    b_ref[...] = jnp.zeros_like(b_ref)
    b_ref[:, :npc] = interp_ref[...]
    interp = b_ref[...]
    parts = split2(interp)
    rows = lax.broadcasted_iota(jnp.int32, (ext, LANE), 0)
    for cell in range(cells):
        cols = slice(cell * LANE, (cell + 1) * LANE)
        hot = (rows == conn_ref[cell : cell + 1, :]).astype(F32).astype(BF16)
        gt_ref[:, cols] = hot
        local = dot3(parts, split2(interp * pot_ref[:, cell : cell + 1]), TN)
        local = local + k_ref[...] * scale_ref[0:1, cell : cell + 1]
        both = part_dot(hot, jnp.concatenate(split2(local), axis=1)).astype(BF16)
        w_ref[0, :, cols] = both[:, :LANE]
        w_ref[1, :, cols] = both[:, LANE:]
    for first in range(0, ext, PAD):
        for second in range(first, ext, PAD):
            here, there = slice(first, first + PAD), slice(second, second + PAD)
            hot = gt_ref[there, :]
            block = part_dot(w_ref[1, here, :], hot, NT) + part_dot(w_ref[0, here, :], hot, NT)
            ah_ref[here, there], al_ref[here, there] = split2(block)
            if second > first:
                ah_ref[there, here], al_ref[there, here] = split2(block.T)
            if first == ext - PAD:
                corner_ref[...] = block


def filter_kernel(ndom, fits, node_dev, rows, *refs):
    spec_ref, v_ref, conn_ref, scale_ref, pot_ref, stiff_ref, interp_ref = refs[:7]
    bottom_ref, mass_ref, occ_ref = refs[7:10]
    outs = 1 if fits else 3
    outputs = refs[10 : 10 + outs]
    scratch = refs[10 + outs :]
    ah_ref, al_ref, edge_block, gt_ref, w_ref, k_ref, b_ref = scratch[:7]
    cur, prev, vb, rb, gslot, rslot, kp, mass_row, bottom_row = scratch[7:16]
    vall, ghosts, occs, gp, rs, gall, vp, qp, work, inverse_ref = scratch[16:26]
    fsend, frecv, rsend, rrecv, ksem, psend, precv, ssend, srecv, gsend, grecv = scratch[26:]
    d = lax.axis_index("dom")
    o = lax.axis_index("orb")
    other = 1 - o
    own = v_ref.shape[0]
    nodes = cur.shape[1]
    cells = conn_ref.shape[0]
    has_prev = d > 0
    has_next = d < ndom - 1
    before = lax.rem(d + ndom - 1, ndom)
    after = lax.rem(d + 1, ndom)

    gslot[...] = jnp.zeros_like(gslot)
    rslot[...] = jnp.zeros_like(rslot)
    kp[...] = jnp.zeros_like(kp)
    ghosts[...] = jnp.zeros_like(ghosts)

    barrier = pltpu.get_barrier_semaphore()
    pl.semaphore_signal(
        barrier, inc=1, device_id={"dom": d, "orb": other}, device_id_type=MESH
    )
    if fits:

        def greet(k, carry):
            pl.semaphore_signal(
                barrier,
                inc=1,
                device_id={"dom": lax.rem(d + k, ndom), "orb": o},
                device_id_type=MESH,
            )
            return carry

        lax.fori_loop(1, ndom, greet, 0)
    else:
        for ok, peer in ((has_prev, before), (has_next, after)):

            @pl.when(ok)
            def _():
                pl.semaphore_signal(
                    barrier, inc=1, device_id={"dom": peer, "orb": o}, device_id_type=MESH
                )

    assemble(
        conn_ref, scale_ref, pot_ref, stiff_ref, interp_ref, ah_ref, al_ref, edge_block, gt_ref, w_ref, k_ref, b_ref
    )
    halfwidth = (spec_ref[1] - spec_ref[0]) / 2.0
    centre = (spec_ref[1] + spec_ref[0]) / 2.0
    cur[...] = jnp.zeros_like(cur)
    cur[:, :node_dev] = v_ref[...]
    mass_row[...] = jnp.ones_like(mass_row)
    mass_row[:, :node_dev] = mass_ref[...]
    bottom_row[...] = jnp.full_like(bottom_row, -1)
    bottom_row[:, : bottom_ref.shape[1]] = bottom_ref[...]
    occs[o] = jnp.broadcast_to(occ_ref[...], occs.shape[1:])
    mass = mass_row[...]
    over_mass = 1.0 / (mass * halfwidth)
    shift = centre / halfwidth
    hot = (
        lax.broadcasted_iota(jnp.int32, (nodes, PAD), 0) == bottom_row[...]
    ).astype(F32).astype(BF16)

    if fits:
        pl.semaphore_wait(barrier, ndom)
    else:
        for ok in (has_prev, has_next):

            @pl.when(ok)
            def _():
                pl.semaphore_wait(barrier, 1)

        pl.semaphore_wait(barrier, 1)

    def remote(src, dst, send, recv, dom, orb):
        return pltpu.make_async_remote_copy(
            src_ref=src,
            dst_ref=dst,
            send_sem=send,
            recv_sem=recv,
            device_id={"dom": dom, "orb": orb},
            device_id_type=MESH,
        )

    some = pl.ds(0, rows)

    def face(step):
        return remote(
            vb.at[step, some], gslot.at[step, some], fsend.at[step], frecv.at[step], before, o
        )

    def rim(step):
        return remote(
            rb.at[step, some], rslot.at[step, some], rsend.at[step], rrecv.at[step], after, o
        )

    corner = remote(edge_block.at[some], kp.at[some], ksem.at[0], ksem.at[1], after, o)

    for step in range(DEG):
        value = cur[...]
        parts = split2(value)
        edge = part_dot(hot, parts[1], TT) + part_dot(hot, parts[0], TT)
        vb[step] = edge

        @pl.when(has_prev)
        def _():
            face(step).start()

        rb[step] = dot3((ah_ref[nodes:, :nodes], al_ref[nodes:, :nodes]), parts, NT)

        @pl.when(has_next)
        def _():
            rim(step).start()

        if step == 0:

            @pl.when(has_next)
            def _():
                corner.start()

            occ_copy = remote(occs.at[o], occs.at[o], psend.at[0], precv.at[0], d, other)
            occ_copy.start()

        total = dot3(parts, (ah_ref[:nodes, :nodes], al_ref[:nodes, :nodes]))
        if step == 0:

            @pl.when(has_prev)
            def _():
                corner.wait_recv()

        extra = dot3(split2(kp[...]), split2(edge))

        @pl.when(has_next)
        def _():
            face(step).wait_recv()

        total = total + dot3(
            split2(gslot[step]), (ah_ref[nodes:, :nodes], al_ref[nodes:, :nodes]), TN
        )

        @pl.when(has_prev)
        def _():
            rim(step).wait_recv()

        total = total + pick_dot(split2(extra + rslot[step]), hot, TT)
        applied = total * over_mass - shift * value
        if step > 0:
            applied = 2.0 * applied - prev[...]
        prev[...] = value
        cur[...] = applied

    value = cur[...]
    vall[o] = value
    half = remote(vall.at[o], vall.at[o], psend.at[1], precv.at[1], d, other)
    half.start()
    parts = split2(value)
    vb[DEG] = part_dot(hot, parts[1], TT) + part_dot(hot, parts[0], TT)

    @pl.when(has_prev)
    def _():
        face(DEG).start()

    weighted = value * mass
    gp[o] = full_dot(weighted, value, NT)
    half.wait_recv()
    gp[other] = full_dot(weighted, vall[other], NT)

    def run(action):
        lax.fori_loop(1, ndom, lambda k, carry: (action(k), carry)[1], 0)

    if fits:
        share = own // ndom
        mine = pl.ds(pl.multiple_of(d * share, 8), share)

        def scatter(k):
            peer = lax.rem(d + k, ndom)
            return remote(
                gp.at[:, pl.ds(pl.multiple_of(peer * share, 8), share), :],
                rs.at[k],
                ssend.at[k],
                srecv.at[k],
                peer,
                o,
            )

        def gather(k):
            return remote(
                gall.at[o, :, mine, :],
                gall.at[o, :, mine, :],
                gsend.at[k],
                grecv.at[k],
                lax.rem(d + k, ndom),
                o,
            )

        def arrive(k):
            came = lax.rem(d + ndom - k, ndom)
            spot = pl.ds(pl.multiple_of(came * share, 8), share)
            return remote(
                gall.at[o, :, spot, :],
                gall.at[o, :, spot, :],
                gsend.at[k],
                grecv.at[k],
                came,
                o,
            )

        run(lambda k: scatter(k).start())

    @pl.when(has_next)
    def _():
        face(DEG).wait_recv()

    ghosts[o] = gslot[DEG]
    ghost = remote(
        ghosts.at[o, some], ghosts.at[o, some], psend.at[2], precv.at[2], d, other
    )
    ghost.start()
    for orb in range(2):
        part = slice(orb * own, (orb + 1) * own)
        vp[0, part, :], vp[1, part, :] = split2(vall[orb])
    ghost.wait_recv()
    far = split2(jnp.concatenate([ghosts[0], ghosts[1]], axis=1))
    basis = split2(b_ref[...])

    def quadrature(first, last):
        for cell in range(first, last):
            cols = slice(cell * LANE, (cell + 1) * LANE)
            local = pick_dot((vp[0], vp[1]), gt_ref[:nodes, cols])
            local = local + pick_dot(far, gt_ref[nodes:, cols], TN)
            qp[0, cell], qp[1, cell] = split2(dot3(split2(local), basis, NT))

    cut = cells // 2
    quadrature(0, cut)
    if fits:
        run(lambda k: scatter(k).wait_recv())
        rs[0] = gp[:, mine, :]
        total = rs[0]
        for k in range(1, ndom):
            total = total + rs[k]
        gall[o, :, mine, :] = total / (ndom * node_dev)
        run(lambda k: gather(k).start())
    quadrature(cut, cells)
    occ_copy.wait_recv()
    if fits:
        run(lambda k: arrive(k).wait_recv())
        swap = remote(gall.at[o], gall.at[o], psend.at[3], precv.at[3], d, other)
        swap.start()
        swap.wait_recv()
        for row in range(2):
            for col in range(2):
                work[row * own : (row + 1) * own, col * own : (col + 1) * own] = gall[row, col]
        finish(work, qp, occs, outputs[0], inverse_ref)
        run(lambda k: scatter(k).wait_send())
        run(lambda k: gather(k).wait_send())
        swap.wait_send()
    else:
        gram_out, q_out, occ_out = outputs
        for row in range(2):
            for col in range(2):
                gram_out[row * own : (row + 1) * own, col * own : (col + 1) * own] = full_dot(
                    vall[row] * mass, vall[col], NT
                )
        q_out[...] = qp[...]
        occ_out[...] = occs[...]

    occ_copy.wait_send()
    half.wait_send()
    ghost.wait_send()
    for step in range(DEG + 1):

        @pl.when(has_prev)
        def _():
            face(step).wait_send()

    for step in range(DEG):

        @pl.when(has_next)
        def _():
            rim(step).wait_send()

    @pl.when(has_next)
    def _():
        corner.wait_send()


def small_inverse(tile, side, size):
    lanes = lax.broadcasted_iota(jnp.int32, tile.shape, 1)
    rows = lax.broadcasted_iota(jnp.int32, tile.shape, 0)
    keep = (lanes >= side * size) & (lanes < (side + 1) * size)
    unit = (lanes - (1 - side) * size == rows).astype(F32)
    work = jnp.where(keep, tile, unit)
    groups = size // 8
    pieces = [work[8 * g : 8 * g + 8] for g in range(groups)]
    below = lax.broadcasted_iota(jnp.int32, (8, LANE), 0)
    panel = 4
    full = (8, LANE)
    for start in range(0, size, panel):
        top, row = divmod(start, 8)
        lane = side * size + start
        head = [pieces[top][row + a : row + a + 1, :] for a in range(panel)]
        line = [jnp.broadcast_to(value, full) for value in head]
        pivot = [
            [
                jnp.broadcast_to(head[a][:, lane + b : lane + b + 1], full) if b >= a else None
                for b in range(panel)
            ]
            for a in range(panel)
        ]
        column = [
            [
                jnp.broadcast_to(pieces[g][:, lane + b : lane + b + 1], full)
                for b in range(panel)
            ]
            for g in range(top, groups)
        ]
        for a in range(panel):
            over = 1.0 / pivot[a][a]
            for g in range(top, groups):
                if g == top and row + a == 7:
                    continue
                terms = column[g - top]
                factor = terms[a] * over
                if g == top:
                    factor = jnp.where(below > row + a, factor, 0.0)
                pieces[g] = pieces[g] - factor * line[a]
                for b in range(a + 1, panel):
                    terms[b] = terms[b] - factor * pivot[a][b]
            for b in range(a + 1, panel):
                factor = pivot[a][b] * over
                line[b] = line[b] - factor * line[a]
                for c in range(b, panel):
                    pivot[b][c] = pivot[b][c] - factor * pivot[a][c]
    work = jnp.concatenate(pieces, axis=0)
    diag = jnp.sum(jnp.where(lanes - side * size == rows, work, 0.0), axis=1, keepdims=True)
    work = work * (1.0 / jnp.sqrt(diag))
    return work[:, (1 - side) * size : (2 - side) * size]


def finish(w_ref, q_ref, occ_ref, out_ref, x_ref):
    orbs = x_ref.shape[0]
    own = occ_ref.shape[2]
    size = 64
    shape = (orbs, orbs)
    eye = lax.broadcasted_iota(jnp.int32, shape, 0) == lax.broadcasted_iota(jnp.int32, shape, 1)
    w_ref[:, orbs:] = eye.astype(F32)
    for first in range(0, orbs, size):
        last = first + size
        base = first // LANE * LANE
        tile = w_ref[first:last, base : base + LANE]
        lower = small_inverse(tile, (first - base) // size, size)
        step = full_dot(lower, w_ref[first:last, :])
        x_ref[first:last, :] = step[:, orbs:]
        if last < orbs:
            w_ref[last:, :] = w_ref[last:, :] - full_dot(step[:, last:orbs], step, TN)
    inverse = split2(x_ref[...])
    occ = jnp.concatenate([occ_ref[0, 0:1, :own], occ_ref[1, 0:1, :own]], axis=1)
    weight = jnp.sum(jnp.where(eye, occ, 0.0), axis=1, keepdims=True) / orbs
    for cell in range(out_ref.shape[0]):
        ortho = dot3(inverse, (q_ref[0, cell], q_ref[1, cell]))
        out_ref[cell : cell + 1, :] = jnp.sum(weight * (ortho * ortho), axis=0, keepdims=True)


def density_kernel(gram_ref, q_ref, occ_ref, out_ref, w_ref, x_ref):
    w_ref[:, : x_ref.shape[0]] = gram_ref[...]
    finish(w_ref, q_ref, occ_ref, out_ref, x_ref)


def per_device(
    ndom, block, conn, bottom, cell_scale, potential, mass, stiffness, interp, occupancy, spectrum
):
    own, node_dev = block.shape
    npc, cells = conn.shape
    gauss = interp.shape[0]
    nodes = up(node_dev, PAD)
    ext = nodes + PAD
    orbs = 2 * own
    rows = up(bottom.shape[0], 8)
    fits = own % (8 * ndom) == 0
    moved = jnp.where(conn >= node_dev, conn + (nodes - node_dev), conn)
    moved = jnp.pad(moved, ((0, LANE - npc), (0, 0)), constant_values=-1).T
    vm = pl.BlockSpec(memory_space=pltpu.VMEM)
    sm = pl.BlockSpec(memory_space=pltpu.SMEM)
    dma = pltpu.SemaphoreType.DMA
    peers = ndom if fits else 1
    share = own // ndom if fits else 8
    density_shape = jax.ShapeDtypeStruct((cells, gauss), F32)
    if fits:
        out_shape = density_shape
    else:
        out_shape = (
            jax.ShapeDtypeStruct((orbs, orbs), F32),
            jax.ShapeDtypeStruct((2, cells, orbs, gauss), BF16),
            jax.ShapeDtypeStruct((2, 8, own), F32),
        )
    buffers = [
        ((ext, ext), BF16),
        ((ext, ext), BF16),
        ((PAD, PAD), F32),
        ((ext, cells * LANE), BF16),
        ((2, ext, cells * LANE), BF16),
        ((LANE, LANE), F32),
        ((gauss, LANE), F32),
        ((own, nodes), F32),
        ((own, nodes), F32),
        ((DEG + 1, PAD, own), F32),
        ((DEG, PAD, own), F32),
        ((DEG + 1, PAD, own), F32),
        ((DEG, PAD, own), F32),
        ((PAD, PAD), F32),
        ((1, nodes), F32),
        ((1, PAD), jnp.int32),
        ((2, own, nodes), F32),
        ((2, PAD, own), F32),
        ((2, 8, own), F32),
        ((2, own, own), F32),
        ((peers, 2, share, own), F32),
        ((2, 2, own, own), F32),
        ((2, orbs, nodes), BF16),
        ((2, cells, orbs, gauss), BF16),
        ((orbs, 2 * orbs), F32),
        ((orbs, orbs), F32),
    ]
    counts = (DEG + 1, DEG + 1, DEG, DEG, 2, 4, 4, peers, peers, peers, peers)
    result = pl.pallas_call(
        functools.partial(filter_kernel, ndom, fits, node_dev, rows),
        name="filter",
        out_shape=out_shape,
        in_specs=[sm] + [vm] * 9,
        out_specs=vm if fits else (vm, vm, vm),
        scratch_shapes=[pltpu.VMEM(*item) for item in buffers] + [dma((n,)) for n in counts],
        compiler_params=pltpu.CompilerParams(
            collective_id=0, has_side_effects=True, vmem_limit_bytes=VLIMIT
        ),
    )(
        spectrum,
        block,
        moved,
        cell_scale[None, :],
        potential,
        stiffness,
        interp,
        bottom[None, :],
        mass[None, :],
        occupancy[None, :],
    )
    if fits:
        return result.T
    gram, quad, occ = result
    gram = lax.psum(gram, "dom") / (ndom * node_dev)
    density = pl.pallas_call(
        density_kernel,
        name="density",
        out_shape=density_shape,
        in_specs=[vm] * 3,
        out_specs=vm,
        scratch_shapes=[pltpu.VMEM((orbs, 2 * orbs), F32), pltpu.VMEM((orbs, orbs), F32)],
        compiler_params=pltpu.CompilerParams(vmem_limit_bytes=VLIMIT),
    )(gram, quad, occ)
    return density.T


def solution(mesh):
    in_specs = (
        P("orb", "dom"),
        P(None, "dom"),
        P("dom"),
        P("dom"),
        P(None, "dom"),
        P("dom"),
        P(),
        P(),
        P("orb"),
        P(),
    )
    out_specs = P(None, "dom")
    return jax.shard_map(
        functools.partial(per_device, mesh.shape["dom"]),
        mesh=mesh,
        in_specs=in_specs,
        out_specs=out_specs,
        check_vma=False,
    )
```

time: 87 us -> 67.2 us (0.77)
  Pallas kernels: 78.9 us -> 62.7 us
  local copies, waits for them, and re-layouts: 7.03 us -> 3.4 us
    pallas_call x3 -> x1, Pallas kernels: 78.9 us -> 62.7 us  [per_device(): pl.pallas_call(functools.partial(filter_kernel, ndom, fits, node_dev, row...]
    unnamed x16 -> x21, local copies, waits for them, and re-layouts: 6.34 us -> 3.39 us
where the time goes in v1:
time: 67.2 us; the launch traced here: 66.3 us
  Pallas kernels  62.7 us (93%)
  local copies, waits for them, and re-layouts  3.4 us (5%)
    pallas_call x1, Pallas kernels, per_device(): pl.pallas_call(functools.partial(filter_kernel, ndom, fits, node_dev, row...  62.7 us
    unnamed x21, local copies, waits for them, and re-layouts  3.39 us

profile of v1, /device:TPU:1, one launch (start us, length us, event | category | flops | bytes accessed | tf_op | source)
XLA Modules:
  0.0 66.3 jit_solution(14338751079757889964)
XLA Ops:
  0.0 0.0 copy-start.8
  0.0 0.0 copy-start.7
  0.0 0.7 %copy-done.8 = f32[676]{0:T(1024)S(1)} copy-done((f32[676]{0:T(1024)S(1)}, f32[676]{0:T(1024)}, u32[]{:S(2)}) %copy-start.8) | copy-done | bytes 2728
  0.7 0.0 copy-done.7
  0.7 0.0 copy-start.6
  0.7 0.7 %copy-done.6 = f32[216,9]{0,1:T(8,128)S(1)} copy-done((f32[216,9]{0,1:T(8,128)S(1)}, f32[216,9]{0,1:T(8,128)}, u32[]{:S(2)}) %copy-start.6) | copy-done | bytes 7800
  1.4 0.1 copy.12.refs_4_
  1.5 0.0 copy-start
  1.5 0.0 copy-start.1
  1.6 0.0 copy-start.2
  1.6 0.0 copy-start.3
  1.6 0.0 copy-start.4
  1.6 0.0 copy-start.5
  1.6 1.2 %copy.11.refs_1_ = f32[128,676]{1,0:T(8,128)S(1)} copy(f32[128,676]{0,1:T(8,128)} %param.10) | data formatting | bytes 692224 | tf_op args[0]
  2.8 0.0 copy-done
  2.8 0.0 copy-done.1
  2.9 0.0 copy-done.2
  2.9 0.0 copy-done.3
  2.9 0.0 copy-done.4
  2.9 0.0 copy-done.5
  2.9 62.7 %filter.1 = f32[9,216]{1,0:T(8,128)S(1)} custom-call(f32[2]{0:T(128)S(1)} %copy-done.3, f32[128,676]{1,0:T(8,128)S(1)} %copy.11.refs_1_, s32[9,128]{1,0:T(8,128)S(1)} %pad_bitcast_fusion.refs_2_, f32[1,9]{1,0:T(1,128)S(1)} %bitcast.8, f32[216,9]{1,0:T(8,128)S(1)} %copy.12.refs_4_, f32[125,125]{1,0:T(8,128)S(1)} %copy-done.1, f32[216,125]{1,0:T(8,128)S(1)} %copy-done, ...), custom_call_target="tpu_custom_call" | custom-call | tf_op jit(solution)/shard_map/filter/pallas_call | solution.py:517
  65.6 0.6 copy.14
  (3 shorter events, 0.0 us)
Async XLA Ops:
  0.0 0.7 %copy-start.8 = (f32[676]{0:T(1024)S(1)}, f32[676]{0:T(1024)}, u32[]{:S(2)}) copy-start(f32[676]{0:T(1024)} %param.15) | copy-start | bytes 8116
  0.0 0.7 %copy-start.7 = (s32[125,9]{0,1:T(8,128)S(1)}, s32[125,9]{0,1:T(8,128)}, u32[]{:S(2)}) copy-start(s32[125,9]{0,1:T(8,128)} %param.11) | copy-start | bytes 13504
  0.7 0.7 %copy-start.6 = (f32[216,9]{0,1:T(8,128)S(1)}, f32[216,9]{0,1:T(8,128)}, u32[]{:S(2)}) copy-start(f32[216,9]{0,1:T(8,128)} %param.14) | copy-start | bytes 23332
  1.5 1.3 %copy-start = (f32[216,125]{1,0:T(8,128)S(1)}, f32[216,125]{1,0:T(8,128)}, u32[]{:S(2)}) copy-start(f32[216,125]{1,0:T(8,128)} %refs_6_.1) | copy-start | bytes 324004
  1.5 1.3 %copy-start.1 = (f32[125,125]{1,0:T(8,128)S(1)}, f32[125,125]{1,0:T(8,128)}, u32[]{:S(2)}) copy-start(f32[125,125]{1,0:T(8,128)} %refs_5_.1) | copy-start | bytes 187504
  1.6 1.3 %copy-start.2 = (s32[169]{0:T(256)S(1)}, s32[169]{0:T(256)}, u32[]{:S(2)}) copy-start(s32[169]{0:T(256)} %param.12) | copy-start | bytes 2032
  1.6 1.3 %copy-start.3 = (f32[2]{0:T(128)S(1)}, f32[2]{0:T(128)}, u32[]{:S(2)}) copy-start(f32[2]{0:T(128)} %refs_0_.1) | copy-start | bytes 28
  1.6 1.3 %copy-start.4 = (f32[9]{0:T(128)S(1)}, f32[9]{0:T(128)}, u32[]{:S(2)}) copy-start(f32[9]{0:T(128)} %param.13) | copy-start | bytes 112
  1.6 1.3 %copy-start.5 = (f32[128]{0:T(128)S(1)}, f32[128]{0:T(128)}, u32[]{:S(2)}) copy-start(f32[128]{0:T(128)} %param.18) | copy-start | bytes 1540

commit v2 on v1

--- a/solution.py
+++ b/solution.py
@@ -49,10 +49,8 @@
     return part_dot(low, onehot, dims) + part_dot(high, onehot, dims)
 
 
-def assemble(
-    conn_ref, scale_ref, pot_ref, stiff_ref, interp_ref, ah_ref, al_ref, corner_ref, gt_ref, w_ref, k_ref, b_ref
-):
-    ext = ah_ref.shape[0]
+def cell_terms(conn_ref, scale_ref, pot_ref, stiff_ref, interp_ref, gt_ref, w_ref, k_ref, b_ref):
+    ext = gt_ref.shape[0]
     cells = conn_ref.shape[0]
     npc = stiff_ref.shape[0]
     k_ref[...] = jnp.zeros_like(k_ref)
@@ -71,16 +69,16 @@
         both = part_dot(hot, jnp.concatenate(split2(local), axis=1)).astype(BF16)
         w_ref[0, :, cols] = both[:, :LANE]
         w_ref[1, :, cols] = both[:, LANE:]
-    for first in range(0, ext, PAD):
-        for second in range(first, ext, PAD):
-            here, there = slice(first, first + PAD), slice(second, second + PAD)
-            hot = gt_ref[there, :]
-            block = part_dot(w_ref[1, here, :], hot, NT) + part_dot(w_ref[0, here, :], hot, NT)
-            ah_ref[here, there], al_ref[here, there] = split2(block)
-            if second > first:
-                ah_ref[there, here], al_ref[there, here] = split2(block.T)
-            if first == ext - PAD:
-                corner_ref[...] = block
+
+
+def assemble(first, second, ah_ref, al_ref, gt_ref, w_ref):
+    here, there = slice(first, first + PAD), slice(second, second + PAD)
+    hot = gt_ref[there, :]
+    block = part_dot(w_ref[1, here, :], hot, NT) + part_dot(w_ref[0, here, :], hot, NT)
+    ah_ref[here, there], al_ref[here, there] = split2(block)
+    if second > first:
+        ah_ref[there, here], al_ref[there, here] = split2(block.T)
+    return block
 
 
 def filter_kernel(ndom, fits, node_dev, rows, *refs):
@@ -91,8 +89,10 @@
     scratch = refs[10 + outs :]
     ah_ref, al_ref, edge_block, gt_ref, w_ref, k_ref, b_ref = scratch[:7]
     cur, prev, vb, rb, gslot, rslot, kp, mass_row, bottom_row = scratch[7:16]
-    vall, ghosts, occs, gp, rs, gall, vp, qp, work, inverse_ref = scratch[16:26]
-    fsend, frecv, rsend, rrecv, ksem, psend, precv, ssend, srecv, gsend, grecv = scratch[26:]
+    vall, ghosts, occs, gp, rs, gall, vp, qp, work, inverse_ref, vin, near = scratch[16:28]
+    (fsend, frecv, rsend, rrecv, ksem, psend, precv, ssend, srecv, gsend, grecv, insem) = (
+        scratch[28:]
+    )
     d = lax.axis_index("dom")
     o = lax.axis_index("orb")
     other = 1 - o
@@ -104,6 +104,8 @@
     before = lax.rem(d + ndom - 1, ndom)
     after = lax.rem(d + 1, ndom)
 
+    fetch = pltpu.make_async_copy(v_ref, vin, insem.at[0])
+    fetch.start()
     gslot[...] = jnp.zeros_like(gslot)
     rslot[...] = jnp.zeros_like(rslot)
     kp[...] = jnp.zeros_like(kp)
@@ -134,13 +136,15 @@
                     barrier, inc=1, device_id={"dom": peer, "orb": o}, device_id_type=MESH
                 )
 
-    assemble(
-        conn_ref, scale_ref, pot_ref, stiff_ref, interp_ref, ah_ref, al_ref, edge_block, gt_ref, w_ref, k_ref, b_ref
-    )
+    cell_terms(
+        conn_ref, scale_ref, pot_ref, stiff_ref, interp_ref, gt_ref, w_ref, k_ref, b_ref
+    )
+    edge_block[...] = assemble(nodes, nodes, ah_ref, al_ref, gt_ref, w_ref)
     halfwidth = (spec_ref[1] - spec_ref[0]) / 2.0
     centre = (spec_ref[1] + spec_ref[0]) / 2.0
     cur[...] = jnp.zeros_like(cur)
-    cur[:, :node_dev] = v_ref[...]
+    fetch.wait()
+    cur[:, :node_dev] = vin[...]
     mass_row[...] = jnp.ones_like(mass_row)
     mass_row[:, :node_dev] = mass_ref[...]
     bottom_row[...] = jnp.full_like(bottom_row, -1)
@@ -188,31 +192,41 @@
 
     corner = remote(edge_block.at[some], kp.at[some], ksem.at[0], ksem.at[1], after, o)
 
+    def send_face(step, parts):
+        vb[step] = part_dot(hot, parts[1], TT) + part_dot(hot, parts[0], TT)
+
+        @pl.when(has_prev)
+        def _():
+            face(step).start()
+
+    def send_rim(step, parts):
+        rb[step] = dot3((ah_ref[nodes:, :nodes], al_ref[nodes:, :nodes]), parts, NT)
+
+        @pl.when(has_next)
+        def _():
+            rim(step).start()
+
+    @pl.when(has_next)
+    def _():
+        corner.start()
+
+    parts = split2(cur[...])
+    send_face(0, parts)
+    occ_copy = remote(occs.at[o], occs.at[o], psend.at[0], precv.at[0], d, other)
+    occ_copy.start()
+    for first in range(0, nodes, PAD):
+        assemble(first, nodes, ah_ref, al_ref, gt_ref, w_ref)
+    send_rim(0, parts)
+    for first in range(0, nodes, PAD):
+        for second in range(first, nodes, PAD):
+            assemble(first, second, ah_ref, al_ref, gt_ref, w_ref)
+
     for step in range(DEG):
         value = cur[...]
         parts = split2(value)
-        edge = part_dot(hot, parts[1], TT) + part_dot(hot, parts[0], TT)
-        vb[step] = edge
-
-        @pl.when(has_prev)
-        def _():
-            face(step).start()
-
-        rb[step] = dot3((ah_ref[nodes:, :nodes], al_ref[nodes:, :nodes]), parts, NT)
-
-        @pl.when(has_next)
-        def _():
-            rim(step).start()
-
-        if step == 0:
-
-            @pl.when(has_next)
-            def _():
-                corner.start()
-
-            occ_copy = remote(occs.at[o], occs.at[o], psend.at[0], precv.at[0], d, other)
-            occ_copy.start()
-
+        if step > 0:
+            send_face(step, parts)
+            send_rim(step, parts)
         total = dot3(parts, (ah_ref[:nodes, :nodes], al_ref[:nodes, :nodes]))
         if step == 0:
 
@@ -220,7 +234,7 @@
             def _():
                 corner.wait_recv()
 
-        extra = dot3(split2(kp[...]), split2(edge))
+        extra = dot3(split2(kp[...]), split2(vb[step]))
 
         @pl.when(has_next)
         def _():
@@ -246,16 +260,11 @@
     half = remote(vall.at[o], vall.at[o], psend.at[1], precv.at[1], d, other)
     half.start()
     parts = split2(value)
-    vb[DEG] = part_dot(hot, parts[1], TT) + part_dot(hot, parts[0], TT)
-
-    @pl.when(has_prev)
-    def _():
-        face(DEG).start()
-
-    weighted = value * mass
-    gp[o] = full_dot(weighted, value, NT)
+    send_face(DEG, parts)
+    weighted = split2(value * mass)
+    gp[o] = dot3(weighted, parts, NT)
     half.wait_recv()
-    gp[other] = full_dot(weighted, vall[other], NT)
+    gp[other] = dot3(weighted, split2(vall[other]), NT)
 
     def run(action):
         lax.fori_loop(1, ndom, lambda k, carry: (action(k), carry)[1], 0)
@@ -299,6 +308,11 @@
 
         run(lambda k: scatter(k).start())
 
+    for orb in range(2):
+        part = slice(orb * own, (orb + 1) * own)
+        vp[0, part, :], vp[1, part, :] = split2(vall[orb])
+    near[...] = pick_dot((vp[0], vp[1]), gt_ref[:nodes, :])
+
     @pl.when(has_next)
     def _():
         face(DEG).wait_recv()
@@ -308,22 +322,6 @@
         ghosts.at[o, some], ghosts.at[o, some], psend.at[2], precv.at[2], d, other
     )
     ghost.start()
-    for orb in range(2):
-        part = slice(orb * own, (orb + 1) * own)
-        vp[0, part, :], vp[1, part, :] = split2(vall[orb])
-    ghost.wait_recv()
-    far = split2(jnp.concatenate([ghosts[0], ghosts[1]], axis=1))
-    basis = split2(b_ref[...])
-
-    def quadrature(first, last):
-        for cell in range(first, last):
-            cols = slice(cell * LANE, (cell + 1) * LANE)
-            local = pick_dot((vp[0], vp[1]), gt_ref[:nodes, cols])
-            local = local + pick_dot(far, gt_ref[nodes:, cols], TN)
-            qp[0, cell], qp[1, cell] = split2(dot3(split2(local), basis, NT))
-
-    cut = cells // 2
-    quadrature(0, cut)
     if fits:
         run(lambda k: scatter(k).wait_recv())
         rs[0] = gp[:, mine, :]
@@ -332,7 +330,13 @@
             total = total + rs[k]
         gall[o, :, mine, :] = total / (ndom * node_dev)
         run(lambda k: gather(k).start())
-    quadrature(cut, cells)
+    ghost.wait_recv()
+    far = split2(jnp.concatenate([ghosts[0], ghosts[1]], axis=1))
+    basis = split2(b_ref[...])
+    for cell in range(cells):
+        cols = slice(cell * LANE, (cell + 1) * LANE)
+        local = near[:, cols] + pick_dot(far, gt_ref[nodes:, cols], TN)
+        qp[0, cell], qp[1, cell] = split2(dot3(split2(local), basis, NT))
     occ_copy.wait_recv()
     if fits:
         run(lambda k: arrive(k).wait_recv())
@@ -441,10 +445,14 @@
         base = first // LANE * LANE
         tile = w_ref[first:last, base : base + LANE]
         lower = small_inverse(tile, (first - base) // size, size)
-        step = full_dot(lower, w_ref[first:last, :])
-        x_ref[first:last, :] = step[:, orbs:]
+        stop = orbs + up(last, LANE)
+        step = full_dot(lower, w_ref[first:last, base:stop])
+        x_ref[first:last, :] = jnp.zeros((size, orbs), F32)
+        x_ref[first:last, : stop - orbs] = step[:, orbs - base :]
         if last < orbs:
-            w_ref[last:, :] = w_ref[last:, :] - full_dot(step[:, last:orbs], step, TN)
+            w_ref[last:, base:stop] = w_ref[last:, base:stop] - full_dot(
+                step[:, last - base : orbs - base], step, TN
+            )
     inverse = split2(x_ref[...])
     occ = jnp.concatenate([occ_ref[0, 0:1, :own], occ_ref[1, 0:1, :own]], axis=1)
     weight = jnp.sum(jnp.where(eye, occ, 0.0), axis=1, keepdims=True) / orbs
@@ -512,13 +520,15 @@
         ((2, cells, orbs, gauss), BF16),
         ((orbs, 2 * orbs), F32),
         ((orbs, orbs), F32),
+        ((own, node_dev), F32),
+        ((orbs, cells * LANE), F32),
     ]
-    counts = (DEG + 1, DEG + 1, DEG, DEG, 2, 4, 4, peers, peers, peers, peers)
+    counts = (DEG + 1, DEG + 1, DEG, DEG, 2, 4, 4, peers, peers, peers, peers, 1)
     result = pl.pallas_call(
         functools.partial(filter_kernel, ndom, fits, node_dev, rows),
         name="filter",
         out_shape=out_shape,
-        in_specs=[sm] + [vm] * 9,
+        in_specs=[sm, pl.BlockSpec(memory_space=pl.ANY)] + [vm] * 8,
         out_specs=vm if fits else (vm, vm, vm),
         scratch_shapes=[pltpu.VMEM(*item) for item in buffers] + [dma((n,)) for n in counts],
         compiler_params=pltpu.CompilerParams(

time: 67.2 us -> 62.6 us (0.932)
  Pallas kernels: 62.7 us -> 58.7 us
    pallas_call x1, Pallas kernels: 62.7 us -> 58.7 us  [per_device(): pl.pallas_call(functools.partial(filter_kernel, ndom, fits, node_dev, row...]
where the time goes in v2:
time: 62.6 us; the launch traced here: 62.2 us
  Pallas kernels  58.7 us (94%)
  local copies, waits for them, and re-layouts  3.4 us (5%)
    pallas_call x1, Pallas kernels, per_device(): pl.pallas_call(functools.partial(filter_kernel, ndom, fits, node_dev, row...  58.7 us
    unnamed x21, local copies, waits for them, and re-layouts  3.39 us

profile of v2, /device:TPU:1, one launch (start us, length us, event | category | flops | bytes accessed | tf_op | source)
XLA Modules:
  0.0 62.2 jit_solution(16972539109211687155)
XLA Ops:
  0.0 0.0 copy-start.8
  0.0 0.0 copy-start.7
  0.0 0.7 %copy-done.8 = f32[676]{0:T(1024)S(1)} copy-done((f32[676]{0:T(1024)S(1)}, f32[676]{0:T(1024)}, u32[]{:S(2)}) %copy-start.8) | copy-done | bytes 2728
  0.7 0.0 copy-done.7
  0.7 0.0 copy-start.6
  0.7 0.7 %copy-done.6 = f32[216,9]{0,1:T(8,128)S(1)} copy-done((f32[216,9]{0,1:T(8,128)S(1)}, f32[216,9]{0,1:T(8,128)}, u32[]{:S(2)}) %copy-start.6) | copy-done | bytes 7800
  1.4 0.1 copy.12.refs_4_
  1.5 0.0 copy-start
  1.5 0.0 copy-start.1
  1.6 0.0 copy-start.2
  1.6 0.0 copy-start.3
  1.6 0.0 copy-start.4
  1.6 0.0 copy-start.5
  1.6 1.2 %copy.11.refs_1_ = f32[128,676]{1,0:T(8,128)S(1)} copy(f32[128,676]{0,1:T(8,128)} %param.10) | data formatting | bytes 692224 | tf_op args[0]
  2.8 0.0 copy-done
  2.8 0.0 copy-done.1
  2.9 0.0 copy-done.2
  2.9 0.0 copy-done.3
  2.9 0.0 copy-done.4
  2.9 0.0 copy-done.5
  2.9 58.7 %filter.1 = f32[9,216]{1,0:T(8,128)S(1)} custom-call(f32[2]{0:T(128)S(1)} %copy-done.3, f32[128,676]{1,0:T(8,128)S(1)} %copy.11.refs_1_, s32[9,128]{1,0:T(8,128)S(1)} %pad_bitcast_fusion.refs_2_, f32[1,9]{1,0:T(1,128)S(1)} %bitcast.8, f32[216,9]{1,0:T(8,128)S(1)} %copy.12.refs_4_, f32[125,125]{1,0:T(8,128)S(1)} %copy-done.1, f32[216,125]{1,0:T(8,128)S(1)} %copy-done, ...), custom_call_target="tpu_custom_call" | custom-call | tf_op jit(solution)/shard_map/filter/pallas_call | solution.py:527
  61.6 0.6 copy.14
  (3 shorter events, 0.0 us)
Async XLA Ops:
  0.0 0.7 %copy-start.8 = (f32[676]{0:T(1024)S(1)}, f32[676]{0:T(1024)}, u32[]{:S(2)}) copy-start(f32[676]{0:T(1024)} %param.15) | copy-start | bytes 8116
  0.0 0.7 %copy-start.7 = (s32[125,9]{0,1:T(8,128)S(1)}, s32[125,9]{0,1:T(8,128)}, u32[]{:S(2)}) copy-start(s32[125,9]{0,1:T(8,128)} %param.11) | copy-start | bytes 13504
  0.7 0.7 %copy-start.6 = (f32[216,9]{0,1:T(8,128)S(1)}, f32[216,9]{0,1:T(8,128)}, u32[]{:S(2)}) copy-start(f32[216,9]{0,1:T(8,128)} %param.14) | copy-start | bytes 23332
  1.5 1.3 %copy-start = (f32[216,125]{1,0:T(8,128)S(1)}, f32[216,125]{1,0:T(8,128)}, u32[]{:S(2)}) copy-start(f32[216,125]{1,0:T(8,128)} %refs_6_.1) | copy-start | bytes 324004
  1.5 1.3 %copy-start.1 = (f32[125,125]{1,0:T(8,128)S(1)}, f32[125,125]{1,0:T(8,128)}, u32[]{:S(2)}) copy-start(f32[125,125]{1,0:T(8,128)} %refs_5_.1) | copy-start | bytes 187504
  1.6 1.3 %copy-start.2 = (s32[169]{0:T(256)S(1)}, s32[169]{0:T(256)}, u32[]{:S(2)}) copy-start(s32[169]{0:T(256)} %param.12) | copy-start | bytes 2032
  1.6 1.3 %copy-start.3 = (f32[2]{0:T(128)S(1)}, f32[2]{0:T(128)}, u32[]{:S(2)}) copy-start(f32[2]{0:T(128)} %refs_0_.1) | copy-start | bytes 28
  1.6 1.3 %copy-start.4 = (f32[9]{0:T(128)S(1)}, f32[9]{0:T(128)}, u32[]{:S(2)}) copy-start(f32[9]{0:T(128)} %param.13) | copy-start | bytes 112
  1.6 1.3 %copy-start.5 = (f32[128]{0:T(128)S(1)}, f32[128]{0:T(128)}, u32[]{:S(2)}) copy-start(f32[128]{0:T(128)} %param.18) | copy-start | bytes 1540

commit v3 on v2

--- a/solution.py
+++ b/solution.py
@@ -90,7 +90,7 @@
     ah_ref, al_ref, edge_block, gt_ref, w_ref, k_ref, b_ref = scratch[:7]
     cur, prev, vb, rb, gslot, rslot, kp, mass_row, bottom_row = scratch[7:16]
     vall, ghosts, occs, gp, rs, gall, vp, qp, work, inverse_ref, vin, near = scratch[16:28]
-    (fsend, frecv, rsend, rrecv, ksem, psend, precv, ssend, srecv, gsend, grecv, insem) = (
+    (fsend, frecv, rsend, rrecv, ksem, psend, precv, ssend, srecv, gsend, grecv, insem, wsend, wrecv) = (
         scratch[28:]
     )
     d = lax.axis_index("dom")
@@ -306,6 +306,17 @@
                 o,
             )
 
+        def forward(k):
+            spot = pl.ds(pl.multiple_of(lax.rem(d + ndom - k, ndom) * share, 8), share)
+            return remote(
+                gall.at[o, :, spot, :],
+                gall.at[o, :, spot, :],
+                wsend.at[k],
+                wrecv.at[k],
+                d,
+                other,
+            )
+
         run(lambda k: scatter(k).start())
 
     for orb in range(2):
@@ -330,6 +341,7 @@
             total = total + rs[k]
         gall[o, :, mine, :] = total / (ndom * node_dev)
         run(lambda k: gather(k).start())
+        forward(0).start()
     ghost.wait_recv()
     far = split2(jnp.concatenate([ghosts[0], ghosts[1]], axis=1))
     basis = split2(b_ref[...])
@@ -339,17 +351,22 @@
         qp[0, cell], qp[1, cell] = split2(dot3(split2(local), basis, NT))
     occ_copy.wait_recv()
     if fits:
-        run(lambda k: arrive(k).wait_recv())
-        swap = remote(gall.at[o], gall.at[o], psend.at[3], precv.at[3], d, other)
-        swap.start()
-        swap.wait_recv()
+
+        def pass_on(k):
+            arrive(k).wait_recv()
+            forward(k).start()
+
+        run(pass_on)
+        run(lambda k: forward(k).wait_recv())
+        forward(0).wait_recv()
         for row in range(2):
             for col in range(2):
                 work[row * own : (row + 1) * own, col * own : (col + 1) * own] = gall[row, col]
         finish(work, qp, occs, outputs[0], inverse_ref)
         run(lambda k: scatter(k).wait_send())
         run(lambda k: gather(k).wait_send())
-        swap.wait_send()
+        run(lambda k: forward(k).wait_send())
+        forward(0).wait_send()
     else:
         gram_out, q_out, occ_out = outputs
         for row in range(2):
@@ -523,7 +540,7 @@
         ((own, node_dev), F32),
         ((orbs, cells * LANE), F32),
     ]
-    counts = (DEG + 1, DEG + 1, DEG, DEG, 2, 4, 4, peers, peers, peers, peers, 1)
+    counts = (DEG + 1, DEG + 1, DEG, DEG, 2, 4, 4, peers, peers, peers, peers, 1, peers, peers)
     result = pl.pallas_call(
         functools.partial(filter_kernel, ndom, fits, node_dev, rows),
         name="filter",

time: 62.6 us -> 62.9 us (level)
  no operation moved by 1% of the time
where the time goes in v3:
time: 62.9 us; the launch traced here: 62.5 us
  Pallas kernels  59 us (94%)
  local copies, waits for them, and re-layouts  3.4 us (5%)
    pallas_call x1, Pallas kernels, per_device(): pl.pallas_call(functools.partial(filter_kernel, ndom, fits, node_dev, row...  59 us
    unnamed x21, local copies, waits for them, and re-layouts  3.39 us

profile of v3, /device:TPU:1, one launch (start us, length us, event | category | flops | bytes accessed | tf_op | source)
XLA Modules:
  0.0 62.5 jit_solution(2486893632794999085)
XLA Ops:
  0.0 0.0 copy-start.8
  0.0 0.0 copy-start.7
  0.0 0.7 %copy-done.8 = f32[676]{0:T(1024)S(1)} copy-done((f32[676]{0:T(1024)S(1)}, f32[676]{0:T(1024)}, u32[]{:S(2)}) %copy-start.8) | copy-done | bytes 2728
  0.7 0.0 copy-done.7
  0.7 0.0 copy-start.6
  0.7 0.7 %copy-done.6 = f32[216,9]{0,1:T(8,128)S(1)} copy-done((f32[216,9]{0,1:T(8,128)S(1)}, f32[216,9]{0,1:T(8,128)}, u32[]{:S(2)}) %copy-start.6) | copy-done | bytes 7800
  1.4 0.1 copy.12.refs_4_
  1.5 0.0 copy-start
  1.5 0.0 copy-start.1
  1.6 0.0 copy-start.2
  1.6 0.0 copy-start.3
  1.6 0.0 copy-start.4
  1.6 0.0 copy-start.5
  1.6 1.2 %copy.11.refs_1_ = f32[128,676]{1,0:T(8,128)S(1)} copy(f32[128,676]{0,1:T(8,128)} %param.10) | data formatting | bytes 692224 | tf_op args[0]
  2.8 0.0 copy-done
  2.8 0.0 copy-done.1
  2.9 0.0 copy-done.2
  2.9 0.0 copy-done.3
  2.9 0.0 copy-done.4
  2.9 0.0 copy-done.5
  2.9 59.0 %filter.1 = f32[9,216]{1,0:T(8,128)S(1)} custom-call(f32[2]{0:T(128)S(1)} %copy-done.3, f32[128,676]{1,0:T(8,128)S(1)} %copy.11.refs_1_, s32[9,128]{1,0:T(8,128)S(1)} %pad_bitcast_fusion.refs_2_, f32[1,9]{1,0:T(1,128)S(1)} %bitcast.8, f32[216,9]{1,0:T(8,128)S(1)} %copy.12.refs_4_, f32[125,125]{1,0:T(8,128)S(1)} %copy-done.1, f32[216,125]{1,0:T(8,128)S(1)} %copy-done, ...), custom_call_target="tpu_custom_call" | custom-call | tf_op jit(solution)/shard_map/filter/pallas_call | solution.py:544
  61.9 0.6 copy.14
  (3 shorter events, 0.0 us)
Async XLA Ops:
  0.0 0.7 %copy-start.8 = (f32[676]{0:T(1024)S(1)}, f32[676]{0:T(1024)}, u32[]{:S(2)}) copy-start(f32[676]{0:T(1024)} %param.15) | copy-start | bytes 8116
  0.0 0.7 %copy-start.7 = (s32[125,9]{0,1:T(8,128)S(1)}, s32[125,9]{0,1:T(8,128)}, u32[]{:S(2)}) copy-start(s32[125,9]{0,1:T(8,128)} %param.11) | copy-start | bytes 13504
  0.7 0.7 %copy-start.6 = (f32[216,9]{0,1:T(8,128)S(1)}, f32[216,9]{0,1:T(8,128)}, u32[]{:S(2)}) copy-start(f32[216,9]{0,1:T(8,128)} %param.14) | copy-start | bytes 23332
  1.5 1.3 %copy-start = (f32[216,125]{1,0:T(8,128)S(1)}, f32[216,125]{1,0:T(8,128)}, u32[]{:S(2)}) copy-start(f32[216,125]{1,0:T(8,128)} %refs_6_.1) | copy-start | bytes 324004
  1.5 1.3 %copy-start.1 = (f32[125,125]{1,0:T(8,128)S(1)}, f32[125,125]{1,0:T(8,128)}, u32[]{:S(2)}) copy-start(f32[125,125]{1,0:T(8,128)} %refs_5_.1) | copy-start | bytes 187504
  1.6 1.3 %copy-start.2 = (s32[169]{0:T(256)S(1)}, s32[169]{0:T(256)}, u32[]{:S(2)}) copy-start(s32[169]{0:T(256)} %param.12) | copy-start | bytes 2032
  1.6 1.3 %copy-start.3 = (f32[2]{0:T(128)S(1)}, f32[2]{0:T(128)}, u32[]{:S(2)}) copy-start(f32[2]{0:T(128)} %refs_0_.1) | copy-start | bytes 28
  1.6 1.3 %copy-start.4 = (f32[9]{0:T(128)S(1)}, f32[9]{0:T(128)}, u32[]{:S(2)}) copy-start(f32[9]{0:T(128)} %param.13) | copy-start | bytes 112
  1.6 1.3 %copy-start.5 = (f32[128]{0:T(128)S(1)}, f32[128]{0:T(128)}, u32[]{:S(2)}) copy-start(f32[128]{0:T(128)} %param.18) | copy-start | bytes 1540

commit v4 on v2

--- a/solution.py
+++ b/solution.py
@@ -389,7 +389,7 @@
     groups = size // 8
     pieces = [work[8 * g : 8 * g + 8] for g in range(groups)]
     below = lax.broadcasted_iota(jnp.int32, (8, LANE), 0)
-    panel = 4
+    panel = 8
     full = (8, LANE)
     for start in range(0, size, panel):
         top, row = divmod(start, 8)

time: 62.6 us -> 59.5 us (0.950)
  Pallas kernels: 58.7 us -> 55.6 us
    pallas_call x1, Pallas kernels: 58.7 us -> 55.6 us  [per_device(): pl.pallas_call(functools.partial(filter_kernel, ndom, fits, node_dev, row...]
where the time goes in v4:
time: 59.5 us; the launch traced here: 59.1 us
  Pallas kernels  55.6 us (93%)
  local copies, waits for them, and re-layouts  3.4 us (6%)
    pallas_call x1, Pallas kernels, per_device(): pl.pallas_call(functools.partial(filter_kernel, ndom, fits, node_dev, row...  55.6 us
    unnamed x21, local copies, waits for them, and re-layouts  3.39 us

profile of v4, /device:TPU:1, one launch (start us, length us, event | category | flops | bytes accessed | tf_op | source)
XLA Modules:
  0.0 59.1 jit_solution(10154570731546897267)
XLA Ops:
  0.0 0.0 copy-start.8
  0.0 0.0 copy-start.7
  0.0 0.7 %copy-done.8 = f32[676]{0:T(1024)S(1)} copy-done((f32[676]{0:T(1024)S(1)}, f32[676]{0:T(1024)}, u32[]{:S(2)}) %copy-start.8) | copy-done | bytes 2728
  0.7 0.0 copy-done.7
  0.7 0.0 copy-start.6
  0.7 0.7 %copy-done.6 = f32[216,9]{0,1:T(8,128)S(1)} copy-done((f32[216,9]{0,1:T(8,128)S(1)}, f32[216,9]{0,1:T(8,128)}, u32[]{:S(2)}) %copy-start.6) | copy-done | bytes 7800
  1.4 0.1 copy.12.refs_4_
  1.5 0.0 copy-start
  1.5 0.0 copy-start.1
  1.6 0.0 copy-start.2
  1.6 0.0 copy-start.3
  1.6 0.0 copy-start.4
  1.6 0.0 copy-start.5
  1.6 1.2 %copy.11.refs_1_ = f32[128,676]{1,0:T(8,128)S(1)} copy(f32[128,676]{0,1:T(8,128)} %param.10) | data formatting | bytes 692224 | tf_op args[0]
  2.8 0.0 copy-done
  2.8 0.0 copy-done.1
  2.9 0.0 copy-done.2
  2.9 0.0 copy-done.3
  2.9 0.0 copy-done.4
  2.9 0.0 copy-done.5
  2.9 55.6 %filter.1 = f32[9,216]{1,0:T(8,128)S(1)} custom-call(f32[2]{0:T(128)S(1)} %copy-done.3, f32[128,676]{1,0:T(8,128)S(1)} %copy.11.refs_1_, s32[9,128]{1,0:T(8,128)S(1)} %pad_bitcast_fusion.refs_2_, f32[1,9]{1,0:T(1,128)S(1)} %bitcast.8, f32[216,9]{1,0:T(8,128)S(1)} %copy.12.refs_4_, f32[125,125]{1,0:T(8,128)S(1)} %copy-done.1, f32[216,125]{1,0:T(8,128)S(1)} %copy-done, ...), custom_call_target="tpu_custom_call" | custom-call | tf_op jit(solution)/shard_map/filter/pallas_call | solution.py:527
  58.5 0.6 %copy.14 = f32[216,9]{0,1:T(8,128)} copy(f32[216,9]{0,1:T(8,128)S(1)} %bitcast.6) | data formatting | bytes 15552
  (3 shorter events, 0.0 us)
Async XLA Ops:
  0.0 0.7 %copy-start.8 = (f32[676]{0:T(1024)S(1)}, f32[676]{0:T(1024)}, u32[]{:S(2)}) copy-start(f32[676]{0:T(1024)} %param.15) | copy-start | bytes 8116
  0.0 0.7 %copy-start.7 = (s32[125,9]{0,1:T(8,128)S(1)}, s32[125,9]{0,1:T(8,128)}, u32[]{:S(2)}) copy-start(s32[125,9]{0,1:T(8,128)} %param.11) | copy-start | bytes 13504
  0.7 0.7 %copy-start.6 = (f32[216,9]{0,1:T(8,128)S(1)}, f32[216,9]{0,1:T(8,128)}, u32[]{:S(2)}) copy-start(f32[216,9]{0,1:T(8,128)} %param.14) | copy-start | bytes 23332
  1.5 1.3 %copy-start = (f32[216,125]{1,0:T(8,128)S(1)}, f32[216,125]{1,0:T(8,128)}, u32[]{:S(2)}) copy-start(f32[216,125]{1,0:T(8,128)} %refs_6_.1) | copy-start | bytes 324004
  1.5 1.3 %copy-start.1 = (f32[125,125]{1,0:T(8,128)S(1)}, f32[125,125]{1,0:T(8,128)}, u32[]{:S(2)}) copy-start(f32[125,125]{1,0:T(8,128)} %refs_5_.1) | copy-start | bytes 187504
  1.6 1.3 %copy-start.2 = (s32[169]{0:T(256)S(1)}, s32[169]{0:T(256)}, u32[]{:S(2)}) copy-start(s32[169]{0:T(256)} %param.12) | copy-start | bytes 2032
  1.6 1.3 %copy-start.3 = (f32[2]{0:T(128)S(1)}, f32[2]{0:T(128)}, u32[]{:S(2)}) copy-start(f32[2]{0:T(128)} %refs_0_.1) | copy-start | bytes 28
  1.6 1.3 %copy-start.4 = (f32[9]{0:T(128)S(1)}, f32[9]{0:T(128)}, u32[]{:S(2)}) copy-start(f32[9]{0:T(128)} %param.13) | copy-start | bytes 112
  1.6 1.3 %copy-start.5 = (f32[128]{0:T(128)S(1)}, f32[128]{0:T(128)}, u32[]{:S(2)}) copy-start(f32[128]{0:T(128)} %param.18) | copy-start | bytes 1540
